TPU v7x, 32 devices: a whole 2x2x4 slice. The times are simulated.
32 devices in a mesh: tm: 16 (over z, y, x), slab: 2 (over core).
Axes of the slice: x: 2, y: 2, z: 4, core: 2. Of those that a mesh axis runs over, the one named last changes fastest.
Arguments:
- c_values: float32 [64, 8, 64, 128], P('tm', 'slab'), may hold values from -2 to 2
- initial: float32 [8, 64, 128], P('slab'), may hold values from -6 to 6
- diffusivity: float32 [8, 64, 128], P('slab'), may hold values from 0.03 to 0.12
- velocity: float32 [3, 8, 64, 128], P(None, 'slab'), may hold values from -0.09 to 0.09
- gains: float32 [64, 8, 64, 128], P('tm', 'slab'), may hold values from 0 to 1, as said below
Outputs:
- corrected: float32 [64, 8, 64, 128], P('tm', 'slab')
Inputs may be any that keep to these rules, and one draw needn't show every extreme that they name: `gains`: each cell's factor over one coarse interval.
All inputs are finite; a program needn't handle non-finite values.
Results may differ from a plain program's by a relative error of at most 0.00002.
Values sent between devices are 32-bit elements; how exact they have to be, the bound alone decides.
A program may use at most 64 MiB of HBM per device.

v0:
```python
import jax
import jax.numpy as jnp
from jax import lax
from jax.sharding import PartitionSpec as P

STEPS = 8


def padded_2(block, sides, width):
    for axis, dim in sides:
        count = lax.axis_size(axis)
        forward = [(i, i + 1) for i in range(count - 1)]
        backward = [(target, source) for source, target in forward]
        low = lax.ppermute(
            lax.slice_in_dim(block, block.shape[dim] - width, None, axis=dim), axis, forward
        )
        high = lax.ppermute(lax.slice_in_dim(block, 0, width, axis=dim), axis, backward)
        block = jnp.concatenate([low, block, high], axis=dim)
    return block


def shifted(value, axis, steps):
    count = lax.axis_size(axis)
    first, last = (max(0, -steps), min(count, count - steps))
    return lax.ppermute(value, axis, [(source, source + steps) for source in range(first, last)])


def entering_2(part, axis, combine, identity):
    place = lax.axis_index(axis)
    gathered = jax.tree.map(lambda a: lax.all_gather(a, axis), part)
    state = jax.tree.map(lambda a, e: jnp.zeros_like(a) + jnp.asarray(e, a.dtype), part, identity)

    def one(step, state):
        return combine(
            state, jax.tree.map(lambda a: lax.dynamic_index_in_dim(a, step, 0, False), gathered)
        )

    return lax.fori_loop(0, place, one, state)


def upwind(speed, center, minus, plus):
    return jnp.maximum(speed, 0.0) * (center - minus) + jnp.minimum(speed, 0.0) * (plus - center)


def advance(padded, diffusivity, velocity):
    center = padded[:, 1:-1]
    lower_z = padded[:, :-2]
    upper_z = padded[:, 2:]
    flat = jnp.pad(center, ((0, 0), (0, 0), (1, 1), (1, 1)))
    lower_x = flat[:, :, :-2, 1:-1]
    upper_x = flat[:, :, 2:, 1:-1]
    lower_y = flat[:, :, 1:-1, :-2]
    upper_y = flat[:, :, 1:-1, 2:]
    laplace = lower_z + upper_z + lower_x + upper_x + lower_y + upper_y - 6.0 * center
    transport = (
        upwind(velocity[0], center, lower_z, upper_z)
        + upwind(velocity[1], center, lower_x, upper_x)
        + upwind(velocity[2], center, lower_y, upper_y)
    )
    return center + diffusivity * laplace - transport


def propagate(field, diffusivity, velocity):
    for step in range(STEPS):
        padded = padded_2(field, (("slab", 1),), 1)
        field = advance(padded, diffusivity, velocity)
    return field


def combine_maps(earlier, later):
    return (earlier[0] * later[0], later[0] * earlier[1] + later[1])


def body(c_values, initial, diffusivity, velocity, gains):
    count = c_values.shape[0]
    is_first = lax.axis_index("tm") == 0
    received = shifted(c_values[-1], "tm", 1)
    previous = jnp.where(is_first, initial, received)
    starts = jnp.concatenate([previous[None], c_values[:-1]], 0)
    ends = propagate(starts, diffusivity, velocity)
    residual = ends - c_values
    error = jnp.zeros_like(initial)
    product = jnp.ones_like(initial)
    for index_k in range(count):
        error = gains[index_k] * error + residual[index_k]
        product = product * gains[index_k]
    identity = (jnp.ones_like(initial), jnp.zeros_like(initial))
    entering = entering_2((product, error), "tm", combine_maps, identity)
    error = entering[1]
    results = []
    for index_k in range(count):
        error = gains[index_k] * error + residual[index_k]
        results.append(c_values[index_k] + error)
    return jnp.stack(results, 0)


def solution(mesh):
    placed = (
        P("tm", "slab", None, None),
        P("slab", None, None),
        P("slab", None, None),
        P(None, "slab", None, None),
        P("tm", "slab", None, None),
    )
    return jax.shard_map(
        body, mesh=mesh, in_specs=placed, out_specs=P("tm", "slab", None, None), check_vma=False
    )
```

profile of v0, /device:TPU:24, one launch (start us, length us, event | category | flops | bytes accessed | tf_op | source)
XLA Modules:
  0.0 206.9 jit_solution(16968508870975273638)
XLA Ops:
  6.5 1.0 slice_bitcast_fusion
  7.5 3.4 %collective-permute-start = (f32[4,64,128]{2,1,0:T(8,128)S(1)}, f32[4,64,128]{2,1,0:T(8,128)S(1)}, u32[]{:S(2)}, u32[]{:S(2)}) collective-permute-start(f32[4,64,128]{2,1,0:T(8,128)S(1)} %slice_bitcast_fusion), channel_id=1, source_target_pairs={{0,2},{2,4},{4,6},{6,8},{8,10},{10,12},{12,14},{14,16},{16,18},{18... | collective-permute-start | bytes 393224 | tf_op jit(solution)/shard_map/ppermute | solution.py:25
  10.9 1.0 slice.296
  12.0 4.5 %collective-permute-done = f32[4,64,128]{2,1,0:T(8,128)S(1)} collective-permute-done((f32[4,64,128]{2,1,0:T(8,128)S(1)}, f32[4,64,128]{2,1,0:T(8,128)S(1)}, u32[]{:S(2)}, u32[]{:S(2)}) %collective-permute-start) | collective-permute-done | bytes 131104 | tf_op jit(solution)/shard_map/ppermute | solution.py:25
  16.5 1.4 collective-permute-start.2
  17.9 3.0 %collective-permute-start.1 = (f32[4,1,64,128]{3,2,1,0:T(8,128)S(1)}, f32[4,1,64,128]{3,2,1,0:T(8,128)S(1)}, u32[]{:S(2)}, u32[]{:S(2)}) collective-permute-start(f32[4,1,64,128]{3,2,1,0:T(8,128)S(1)} %get-tuple-element.82), channel_id=1, source_target_pairs={{0,1},{2,3},{4,5},{6,7},{8,9},{10,11},{12,13},{14,15},{16,17},{18,... | collective-permute-start | bytes 393224 | tf_op jit(solution)/shard_map/ppermute | solution.py:14
  21.1 0.8 collective-permute-done.1
  21.9 0.6 add_subtract_fusion
  22.6 2.3 %collective-permute-start.3 = (f32[4,1,64,128]{3,2,1,0:T(8,128)S(1)}, f32[4,1,64,128]{3,2,1,0:T(8,128)S(1)}, u32[]{:S(2)}, u32[]{:S(2)}) collective-permute-start(f32[4,1,64,128]{3,2,1,0:T(8,128)S(1)} %get-tuple-element.79), channel_id=1, source_target_pairs={{0,1},{2,3},{4,5},{6,7},{8,9},{10,11},{12,13},{14,15},{16,17},{18,... | collective-permute-start | bytes 393224 | tf_op jit(solution)/shard_map/ppermute | solution.py:14
  24.9 1.3 collective-permute-start.4
  26.2 1.9 collective-permute-done.4
  28.8 2.1 collective-permute-start.5
  30.8 1.3 collective-permute-start.6
  32.1 1.9 collective-permute-done.6
  34.7 2.1 collective-permute-start.7
  36.8 1.3 collective-permute-start.8
  38.1 1.9 collective-permute-done.8
  40.6 2.1 collective-permute-start.9
  42.7 1.3 collective-permute-start.10
  44.0 1.9 collective-permute-done.10
  46.6 2.1 collective-permute-start.11
  48.7 1.3 collective-permute-start.12
  50.0 1.9 collective-permute-done.12
  52.5 2.1 collective-permute-start.13
  54.6 1.4 collective-permute-start.14
  56.1 1.9 collective-permute-done.14
  58.6 2.1 collective-permute-start.15
  60.7 1.4 collective-permute-start.16
  62.1 1.9 collective-permute-done.16
  64.1 0.6 fusion.7
  64.7 0.8 multiply_add_fusion
  65.5 0.7 all-gather.3.cloned.1.call-update
  66.2 57.9 %all-gather.5.cloned.1.call-done = f32[16,4,64,128]{3,2,1,0:T(8,128)} async-done(((f32[1,4,64,128]{3,2,1,0:T(8,128)}), f32[16,4,64,128]{3,2,1,0:T(8,128)}) %all-gather.5.cloned.1.call-update) | async-done | bytes 2097168 | tf_op jit(solution)/shard_map/all_gather | solution.py:30
  124.2 62.2 %all-gather.3.cloned.1.call-done = f32[16,4,64,128]{3,2,1,0:T(8,128)} async-done(((f32[1,4,64,128]{3,2,1,0:T(8,128)}), f32[16,4,64,128]{3,2,1,0:T(8,128)}) %all-gather.3.cloned.1.call-update) | async-done | bytes 2097168 | tf_op jit(solution)/shard_map/all_gather | solution.py:30
  186.4 12.7 %while.12 = (s32[]{:T(128)}, f32[4,64,128]{2,1,0:T(8,128)S(1)}, s32[]{:T(128)}, f32[16,4,64,128]{3,2,1,0:T(8,128)}, f32[16,4,64,128]{3,2,1,0:T(8,128)}, /*index=5*/s32[]{:T(128)}, s32[]{:T(128)}, s32[]{:T(128)}) while((s32[]{:T(128)}, f32[4,64,128]{2,1,0:T(8,128)S(1)}, s32[]{:T(128)}, f32[16,4,64,128]{3,2,1,0:T(8,128)}, ...), condition=%wide.region_1.2_spmd, body=%wide.region_0.1_spmd.sunk | while | flops 65541 | bytes 524419 | solution.py:38
  186.4 1.0 bitcast_add_fusion.10
  187.4 1.0 bitcast_add_fusion.10
  188.5 1.0 bitcast_add_fusion.10
  189.6 1.0 bitcast_add_fusion.10
  190.6 1.0 bitcast_add_fusion.10
  191.7 1.0 bitcast_add_fusion.10
  192.7 1.0 bitcast_add_fusion.10
  193.8 1.0 bitcast_add_fusion.10
  194.8 1.0 bitcast_add_fusion.10
  195.9 1.0 bitcast_add_fusion.10
  197.0 1.0 bitcast_add_fusion.10
  198.0 1.0 bitcast_add_fusion.10
  199.2 0.8 pad_maximum_fusion.19
  (39 shorter events, 4.2 us)
Async XLA Ops:
  6.5 14.4 %copy-start.3 = (f32[3,4,64,128]{3,2,1,0:T(8,128)S(1)}, f32[3,4,64,128]{3,2,1,0:T(8,128)}, u32[]{:S(2)}) copy-start(f32[3,4,64,128]{3,2,1,0:T(8,128)} %param.10) | copy-start | bytes 1179652
  6.5 117.6 %all-gather.5.cloned.1.call-start = ((), (), s32[]{:S(2)}) async-start(), calls=%async_computation.1 | async-start | bytes 2228224 | tf_op jit(solution)/shard_map/all_gather | solution.py:30
  7.5 8.9 %collective-permute-start = (f32[4,64,128]{2,1,0:T(8,128)S(1)}, f32[4,64,128]{2,1,0:T(8,128)S(1)}, u32[]{:S(2)}, u32[]{:S(2)}) collective-permute-start(f32[4,64,128]{2,1,0:T(8,128)S(1)} %slice_bitcast_fusion), channel_id=1, source_target_pairs={{0,2},{2,4},{4,6},{6,8},{8,10},{10,12},{12,14},{14,16},{16,18},{18... | collective-permute-start | bytes 393224 | tf_op jit(solution)/shard_map/ppermute | solution.py:25
  16.5 5.5 %copy-start = (f32[4,64,128]{2,1,0:T(8,128)S(1)}, f32[4,64,128]{2,1,0:T(8,128)}, u32[]{:S(2)}) copy-start(f32[4,64,128]{2,1,0:T(8,128)} %param.9) | copy-start | bytes 393220
  16.5 4.6 %collective-permute-start.2 = (f32[4,1,64,128]{3,2,1,0:T(8,128)S(1)}, f32[4,1,64,128]{3,2,1,0:T(8,128)S(1)}, u32[]{:S(2)}, u32[]{:S(2)}) collective-permute-start(f32[4,1,64,128]{3,2,1,0:T(8,128)S(1)} %get-tuple-element.81), channel_id=1, source_target_pairs={{1,0},{3,2},{5,4},{7,6},{9,8},{11,10},{13,12},{15,14},{17,16},{19,... | collective-permute-start | bytes 393224 | tf_op jit(solution)/shard_map/ppermute | solution.py:17
  17.9 4.0 %collective-permute-start.1 = (f32[4,1,64,128]{3,2,1,0:T(8,128)S(1)}, f32[4,1,64,128]{3,2,1,0:T(8,128)S(1)}, u32[]{:S(2)}, u32[]{:S(2)}) collective-permute-start(f32[4,1,64,128]{3,2,1,0:T(8,128)S(1)} %get-tuple-element.82), channel_id=1, source_target_pairs={{0,1},{2,3},{4,5},{6,7},{8,9},{10,11},{12,13},{14,15},{16,17},{18,... | collective-permute-start | bytes 393224 | tf_op jit(solution)/shard_map/ppermute | solution.py:14
  22.6 3.6 %collective-permute-start.3 = (f32[4,1,64,128]{3,2,1,0:T(8,128)S(1)}, f32[4,1,64,128]{3,2,1,0:T(8,128)S(1)}, u32[]{:S(2)}, u32[]{:S(2)}) collective-permute-start(f32[4,1,64,128]{3,2,1,0:T(8,128)S(1)} %get-tuple-element.79), channel_id=1, source_target_pairs={{0,1},{2,3},{4,5},{6,7},{8,9},{10,11},{12,13},{14,15},{16,17},{18,... | collective-permute-start | bytes 393224 | tf_op jit(solution)/shard_map/ppermute | solution.py:14
  24.9 3.2 %collective-permute-start.4 = (f32[4,1,64,128]{3,2,1,0:T(8,128)S(1)}, f32[4,1,64,128]{3,2,1,0:T(8,128)S(1)}, u32[]{:S(2)}, u32[]{:S(2)}) collective-permute-start(f32[4,1,64,128]{3,2,1,0:T(8,128)S(1)} %get-tuple-element.80), channel_id=1, source_target_pairs={{1,0},{3,2},{5,4},{7,6},{9,8},{11,10},{13,12},{15,14},{17,16},{19,... | collective-permute-start | bytes 393224 | tf_op jit(solution)/shard_map/ppermute | solution.py:17
  28.8 3.4 %collective-permute-start.5 = (f32[4,1,64,128]{3,2,1,0:T(8,128)S(1)}, f32[4,1,64,128]{3,2,1,0:T(8,128)S(1)}, u32[]{:S(2)}, u32[]{:S(2)}) collective-permute-start(f32[4,1,64,128]{3,2,1,0:T(8,128)S(1)} %get-tuple-element.77), channel_id=1, source_target_pairs={{0,1},{2,3},{4,5},{6,7},{8,9},{10,11},{12,13},{14,15},{16,17},{18,... | collective-permute-start | bytes 393224 | tf_op jit(solution)/shard_map/ppermute | solution.py:14
  30.8 3.2 %collective-permute-start.6 = (f32[4,1,64,128]{3,2,1,0:T(8,128)S(1)}, f32[4,1,64,128]{3,2,1,0:T(8,128)S(1)}, u32[]{:S(2)}, u32[]{:S(2)}) collective-permute-start(f32[4,1,64,128]{3,2,1,0:T(8,128)S(1)} %get-tuple-element.78), channel_id=1, source_target_pairs={{1,0},{3,2},{5,4},{7,6},{9,8},{11,10},{13,12},{15,14},{17,16},{19,... | collective-permute-start | bytes 393224 | tf_op jit(solution)/shard_map/ppermute | solution.py:17
  34.7 3.4 %collective-permute-start.7 = (f32[4,1,64,128]{3,2,1,0:T(8,128)S(1)}, f32[4,1,64,128]{3,2,1,0:T(8,128)S(1)}, u32[]{:S(2)}, u32[]{:S(2)}) collective-permute-start(f32[4,1,64,128]{3,2,1,0:T(8,128)S(1)} %get-tuple-element.75), channel_id=1, source_target_pairs={{0,1},{2,3},{4,5},{6,7},{8,9},{10,11},{12,13},{14,15},{16,17},{18,... | collective-permute-start | bytes 393224 | tf_op jit(solution)/shard_map/ppermute | solution.py:14
  36.8 3.2 %collective-permute-start.8 = (f32[4,1,64,128]{3,2,1,0:T(8,128)S(1)}, f32[4,1,64,128]{3,2,1,0:T(8,128)S(1)}, u32[]{:S(2)}, u32[]{:S(2)}) collective-permute-start(f32[4,1,64,128]{3,2,1,0:T(8,128)S(1)} %get-tuple-element.76), channel_id=1, source_target_pairs={{1,0},{3,2},{5,4},{7,6},{9,8},{11,10},{13,12},{15,14},{17,16},{19,... | collective-permute-start | bytes 393224 | tf_op jit(solution)/shard_map/ppermute | solution.py:17
  40.6 3.4 %collective-permute-start.9 = (f32[4,1,64,128]{3,2,1,0:T(8,128)S(1)}, f32[4,1,64,128]{3,2,1,0:T(8,128)S(1)}, u32[]{:S(2)}, u32[]{:S(2)}) collective-permute-start(f32[4,1,64,128]{3,2,1,0:T(8,128)S(1)} %get-tuple-element.73), channel_id=1, source_target_pairs={{0,1},{2,3},{4,5},{6,7},{8,9},{10,11},{12,13},{14,15},{16,17},{18,... | collective-permute-start | bytes 393224 | tf_op jit(solution)/shard_map/ppermute | solution.py:14
  42.7 3.2 %collective-permute-start.10 = (f32[4,1,64,128]{3,2,1,0:T(8,128)S(1)}, f32[4,1,64,128]{3,2,1,0:T(8,128)S(1)}, u32[]{:S(2)}, u32[]{:S(2)}) collective-permute-start(f32[4,1,64,128]{3,2,1,0:T(8,128)S(1)} %get-tuple-element.74), channel_id=1, source_target_pairs={{1,0},{3,2},{5,4},{7,6},{9,8},{11,10},{13,12},{15,14},{17,16},{19,... | collective-permute-start | bytes 393224 | tf_op jit(solution)/shard_map/ppermute | solution.py:17
  46.6 3.4 %collective-permute-start.11 = (f32[4,1,64,128]{3,2,1,0:T(8,128)S(1)}, f32[4,1,64,128]{3,2,1,0:T(8,128)S(1)}, u32[]{:S(2)}, u32[]{:S(2)}) collective-permute-start(f32[4,1,64,128]{3,2,1,0:T(8,128)S(1)} %get-tuple-element.71), channel_id=1, source_target_pairs={{0,1},{2,3},{4,5},{6,7},{8,9},{10,11},{12,13},{14,15},{16,17},{18,... | collective-permute-start | bytes 393224 | tf_op jit(solution)/shard_map/ppermute | solution.py:14
  48.7 3.2 %collective-permute-start.12 = (f32[4,1,64,128]{3,2,1,0:T(8,128)S(1)}, f32[4,1,64,128]{3,2,1,0:T(8,128)S(1)}, u32[]{:S(2)}, u32[]{:S(2)}) collective-permute-start(f32[4,1,64,128]{3,2,1,0:T(8,128)S(1)} %get-tuple-element.72), channel_id=1, source_target_pairs={{1,0},{3,2},{5,4},{7,6},{9,8},{11,10},{13,12},{15,14},{17,16},{19,... | collective-permute-start | bytes 393224 | tf_op jit(solution)/shard_map/ppermute | solution.py:17
  52.5 3.5 %collective-permute-start.13 = (f32[4,1,64,128]{3,2,1,0:T(8,128)S(1)}, f32[4,1,64,128]{3,2,1,0:T(8,128)S(1)}, u32[]{:S(2)}, u32[]{:S(2)}) collective-permute-start(f32[4,1,64,128]{3,2,1,0:T(8,128)S(1)} %get-tuple-element.69), channel_id=1, source_target_pairs={{0,1},{2,3},{4,5},{6,7},{8,9},{10,11},{12,13},{14,15},{16,17},{18,... | collective-permute-start | bytes 393224 | tf_op jit(solution)/shard_map/ppermute | solution.py:14
  54.6 9.5 %copy-start.1 = (f32[4,4,64,128]{3,2,1,0:T(8,128)S(1)}, f32[4,4,64,128]{3,2,1,0:T(8,128)}, u32[]{:S(2)}) copy-start(f32[4,4,64,128]{3,2,1,0:T(8,128)} %param.7) | copy-start | bytes 1572868
  54.6 3.4 %collective-permute-start.14 = (f32[4,1,64,128]{3,2,1,0:T(8,128)S(1)}, f32[4,1,64,128]{3,2,1,0:T(8,128)S(1)}, u32[]{:S(2)}, u32[]{:S(2)}) collective-permute-start(f32[4,1,64,128]{3,2,1,0:T(8,128)S(1)} %get-tuple-element.70), channel_id=1, source_target_pairs={{1,0},{3,2},{5,4},{7,6},{9,8},{11,10},{13,12},{15,14},{17,16},{19,... | collective-permute-start | bytes 393224 | tf_op jit(solution)/shard_map/ppermute | solution.py:17
  58.6 3.5 %collective-permute-start.15 = (f32[4,1,64,128]{3,2,1,0:T(8,128)S(1)}, f32[4,1,64,128]{3,2,1,0:T(8,128)S(1)}, u32[]{:S(2)}, u32[]{:S(2)}) collective-permute-start(f32[4,1,64,128]{3,2,1,0:T(8,128)S(1)} %get-tuple-element.67), channel_id=1, source_target_pairs={{0,1},{2,3},{4,5},{6,7},{8,9},{10,11},{12,13},{14,15},{16,17},{18,... | collective-permute-start | bytes 393224 | tf_op jit(solution)/shard_map/ppermute | solution.py:14
  60.7 4.0 %copy-start.2 = (f32[4,4,64,128]{3,2,1,0:T(8,128)S(1)}, f32[4,4,64,128]{3,2,1,0:T(8,128)}, u32[]{:S(2)}) copy-start(f32[4,4,64,128]{3,2,1,0:T(8,128)} %param.11) | copy-start | bytes 1572868
  60.7 3.4 %collective-permute-start.16 = (f32[4,1,64,128]{3,2,1,0:T(8,128)S(1)}, f32[4,1,64,128]{3,2,1,0:T(8,128)S(1)}, u32[]{:S(2)}, u32[]{:S(2)}) collective-permute-start(f32[4,1,64,128]{3,2,1,0:T(8,128)S(1)} %get-tuple-element.68), channel_id=1, source_target_pairs={{1,0},{3,2},{5,4},{7,6},{9,8},{11,10},{13,12},{15,14},{17,16},{19,... | collective-permute-start | bytes 393224 | tf_op jit(solution)/shard_map/ppermute | solution.py:17
  65.5 120.8 %all-gather.3.cloned.1.call-start = ((), (), s32[]{:S(2)}) async-start(), calls=%async_computation | async-start | bytes 2228224 | tf_op jit(solution)/shard_map/all_gather | solution.py:30
Sparse Core Ops, SparseCore 0:
  65.6 58.5 all-gather.4
  127.0 59.3 all-gather.2
where the time goes:
time: 210 us; the launch traced here: 207 us
  waiting for transfers between devices  140 us (67%)
  starting transfers between devices  31.8 us (15%)
  other arithmetic  19.2 us (9%)
  between operations  13.8 us (7%)
  local copies, waits for them, and re-layouts  2.16 us (1%)
    all_gather x2, waiting for transfers between devices, entering_2(): gathered = jax.tree.map(lambda a: lax.all_gather(a, axis), part)  120 us
    ppermute x8, starting transfers between devices, padded_2(): lax.ppermute(lax.slice_in_dim(block, block.shape[dim] - width, None, axis...  17.7 us
    ppermute x8, waiting for transfers between devices, padded_2(): lax.ppermute(lax.slice_in_dim(block, 0, width, axis=dim), axis, backward)  13.5 us
    add x12, other arithmetic, combine_maps(): return (earlier[0] * later[0], later[0] * earlier[1] + later[1])  12.5 us
    ppermute x8, starting transfers between devices, padded_2(): lax.ppermute(lax.slice_in_dim(block, 0, width, axis=dim), axis, backward)  10.7 us
    ppermute x1, waiting for transfers between devices, shifted(): lax.ppermute(value, axis, [(source, source + steps) for source in range(f...  4.48 us
    sub x7, other arithmetic, advance(): return center + diffusivity * laplace - transport  4.25 us
  transfers between devices with their start and end apart: 19, of which 11 were waited for; matrix products, arithmetic and copies ran while one was open for 1% of the time, Pallas kernels for 0%

commit v1 on v0

--- a/solution.py
+++ b/solution.py
@@ -1,9 +1,14 @@
+import functools
+
 import jax
 import jax.numpy as jnp
 from jax import lax
+from jax.experimental import pallas as pl
+from jax.experimental.pallas import tpu as pltpu
 from jax.sharding import PartitionSpec as P
 
 STEPS = 8
+MESH = pl.DeviceIdType.MESH
 
 
 def padded_2(block, sides, width):
@@ -94,6 +99,391 @@
     return jnp.stack(results, 0)
 
 
+def fused_kernel(
+    n, nx, half,
+    c_hbm, init_hbm, diff_hbm, vel_hbm, gains_hbm, out_ref,
+    c_own, g_own, raw, coef, first, second, spare, ends,
+    base, cum, block_e, all_p, all_e, leave, enter,
+    local_sem, swap_send, swap_recv, start_send, start_recv, ends_send, ends_recv,
+    p_send, p_recv, e_send, e_recv, x_send, x_recv,
+):
+    t, s = lax.axis_index("tm"), lax.axis_index("slab")
+    other = 1 - s
+    lanes = c_own.shape[-1]
+    planes = half // nx
+    whole = 2 * half
+    part = half // n
+    mine = pl.ds(pl.multiple_of(s * half, half), half)
+    theirs = pl.ds(pl.multiple_of(other * half, half), half)
+    mine_in = pl.ds(pl.multiple_of(nx + s * half, nx), half)
+    theirs_in = pl.ds(pl.multiple_of(nx + other * half, nx), half)
+
+    barrier = pltpu.get_barrier_semaphore()
+
+    def greet(where):
+        pl.semaphore_signal(barrier, inc=1, device_id=where, device_id_type=MESH)
+
+    def hello(d, carry):
+        greet((lax.rem(t + d, n), s))
+        return carry
+
+    zero = jnp.zeros((nx, lanes), jnp.float32)
+    for field in (first, second, spare):
+        field[0:nx] = zero
+        field[nx + whole : 2 * nx + whole] = zero
+
+    greet((t, other))
+
+    @pl.when((s == 0) & (t > 0))
+    def _():
+        greet((t - 1, other))
+
+    @pl.when((s == 1) & (t < n - 1))
+    def _():
+        greet((t + 1, other))
+
+    lax.fori_loop(1, n, hello, 0)
+
+    local_diff = pltpu.make_async_copy(diff_hbm, raw.at[0, mine], local_sem.at[0])
+    local_vel = pltpu.make_async_copy(vel_hbm, raw.at[1:4, mine], local_sem.at[1])
+    local_c = pltpu.make_async_copy(c_hbm, c_own, local_sem.at[2])
+    local_g = pltpu.make_async_copy(gains_hbm, g_own, local_sem.at[3])
+    local_first = pltpu.make_async_copy(c_hbm.at[2 * s], first.at[mine_in], local_sem.at[4])
+    local_second = pltpu.make_async_copy(c_hbm.at[1], second.at[mine_in], local_sem.at[5])
+    local_init = pltpu.make_async_copy(init_hbm, second.at[mine_in], local_sem.at[6])
+    local_diff.start()
+    local_vel.start()
+    local_first.start()
+
+    @pl.when(s == 1)
+    def _():
+        local_second.start()
+
+    @pl.when((s == 0) & (t == 0))
+    def _():
+        local_init.start()
+
+    local_g.start()
+    local_c.start()
+
+    extra = jnp.where(s == 0, jnp.where(t > 0, 1, 0), jnp.where(t < n - 1, 1, 0))
+    pl.semaphore_wait(barrier, n + extra)
+
+    def remote(src, dst, send, recv, where):
+        return pltpu.make_async_remote_copy(
+            src_ref=src, dst_ref=dst, send_sem=send, recv_sem=recv,
+            device_id=where, device_id_type=MESH,
+        )
+
+    swap_first = remote(
+        c_hbm.at[2 * other], first.at[mine_in], swap_send.at[0], swap_recv.at[0], (t, other)
+    )
+    swap_diff = remote(diff_hbm, raw.at[0, mine], swap_send.at[1], swap_recv.at[1], (t, other))
+    swap_vel = remote(vel_hbm, raw.at[1:4, mine], swap_send.at[2], swap_recv.at[2], (t, other))
+    to_next = remote(
+        c_hbm.at[3], second.at[mine_in], start_send.at[0], start_recv.at[s], (t + 1, 0)
+    )
+    to_upper = remote(
+        c_hbm.at[1], second.at[mine_in], start_send.at[1], start_recv.at[s], (t, 1)
+    )
+    to_lower = remote(
+        init_hbm, second.at[mine_in], start_send.at[2], start_recv.at[s], (t, 0)
+    )
+
+    @pl.when(t < n - 1)
+    def _():
+        to_next.start()
+
+    swap_diff.start()
+    swap_vel.start()
+    swap_first.start()
+
+    @pl.when(s == 0)
+    def _():
+        to_upper.start()
+
+    @pl.when((s == 1) & (t == 0))
+    def _():
+        to_lower.start()
+
+    row = lax.broadcasted_iota(jnp.int32, (nx, lanes), 0)
+    lane = lax.broadcasted_iota(jnp.int32, (nx, lanes), 1)
+
+    def coefficients(start):
+        def plane(z, carry):
+            at = pl.ds(pl.multiple_of(start + z * nx, nx), nx)
+            d = raw[0, at]
+            centre = 1.0 - 6.0 * d
+            for q in range(3):
+                speed = raw[q + 1, at]
+                up = jnp.maximum(speed, 0.0)
+                down = jnp.minimum(speed, 0.0)
+                centre = centre - up + down
+                minus = d + up
+                plus = d - down
+                if q == 1:
+                    minus = jnp.where(row == 0, 0.0, minus)
+                    plus = jnp.where(row == nx - 1, 0.0, plus)
+                if q == 2:
+                    minus = jnp.where(lane == 0, 0.0, minus)
+                    plus = jnp.where(lane == lanes - 1, 0.0, plus)
+                coef[1 + 2 * q, at] = minus
+                coef[2 + 2 * q, at] = plus
+            coef[0, at] = centre
+            return carry
+
+        lax.fori_loop(0, planes, plane, 0)
+
+    local_diff.wait()
+    local_vel.wait()
+    coefficients(s * half)
+
+    local_g.wait()
+
+    def products(z, carry):
+        at = pl.ds(pl.multiple_of(z * nx, nx), nx)
+        p = g_own[0, at]
+        cum[0, at] = p
+        for k in range(1, 4):
+            p = p * g_own[k, at]
+            cum[k, at] = p
+        return carry
+
+    lax.fori_loop(0, planes, products, 0)
+
+    def share(q):
+        return pl.ds(pl.multiple_of(q * part, part), part)
+
+    def p_copy(peer, index):
+        return remote(
+            cum.at[3, share(peer)], all_p.at[t], p_send.at[index], p_recv.at[t], (peer, s)
+        )
+
+    def e_copy(peer, index):
+        return remote(
+            block_e.at[share(peer)], all_e.at[t], e_send.at[index], e_recv.at[t], (peer, s)
+        )
+
+    def x_copy(peer, index):
+        return remote(
+            leave.at[peer], enter.at[share(t)], x_send.at[index], x_recv.at[t], (peer, s)
+        )
+
+    def send_all(copy):
+        def one(d, carry):
+            copy(lax.rem(t + d, n), d).start()
+            return carry
+
+        lax.fori_loop(1, n, one, 0)
+
+    swap_diff.wait_recv()
+    swap_vel.wait_recv()
+    coefficients(other * half)
+
+    def step(src, dst):
+        for z in range(2 * planes):
+            at = nx + z * nx
+            here = z * nx
+            v = src[at : at + nx]
+            new = coef[0, here : here + nx] * v
+            new += coef[1, here : here + nx] * src[at - nx : at]
+            new += coef[2, here : here + nx] * src[at + nx : at + 2 * nx]
+            new += coef[3, here : here + nx] * src[at - 1 : at + nx - 1]
+            new += coef[4, here : here + nx] * src[at + 1 : at + nx + 1]
+            new += coef[5, here : here + nx] * pltpu.roll(v, 1, 1)
+            new += coef[6, here : here + nx] * pltpu.roll(v, lanes - 1, 1)
+            dst[at : at + nx] = new
+
+    def propagated(field):
+        def pair(i, carry):
+            step(field, spare)
+            step(spare, field)
+            return carry
+
+        lax.fori_loop(0, STEPS // 2, pair, 0)
+
+    local_first.wait()
+    swap_first.wait_recv()
+    send_all(p_copy)
+    propagated(first)
+
+    back_first = remote(
+        first.at[theirs_in], ends.at[1], ends_send.at[0], ends_recv.at[0], (t, other)
+    )
+    back_first.start()
+
+    @pl.when(s == 1)
+    def _():
+        local_second.wait()
+
+    @pl.when((s == 0) & (t == 0))
+    def _():
+        local_init.wait()
+
+    @pl.when((s == 1) | (t > 0))
+    def _():
+        remote(
+            c_hbm.at[3], second.at[nx : nx + half], start_send.at[0], start_recv.at[0], (t, other)
+        ).wait_recv()
+
+    @pl.when(s == 0)
+    def _():
+        remote(
+            c_hbm.at[3], second.at[nx + half : nx + whole],
+            start_send.at[0], start_recv.at[1], (t, other),
+        ).wait_recv()
+
+    propagated(second)
+    back_second = remote(
+        second.at[theirs_in], ends.at[0], ends_send.at[1], ends_recv.at[1], (t, other)
+    )
+    back_second.start()
+    local_c.wait()
+    back_first.wait_recv()
+    back_second.wait_recv()
+
+    def local_errors(lower):
+        def plane(z, carry):
+            at = pl.ds(pl.multiple_of(z * nx, nx), nx)
+            own_at = pl.ds(pl.multiple_of(nx + s * half + z * nx, nx), nx)
+            own = [second[own_at], first[own_at]]
+            got = [ends[0, at], ends[1, at]]
+            finals = own + got if lower else got + own
+            error = jnp.zeros((nx, lanes), jnp.float32)
+            for k in range(4):
+                c = c_own[k, at]
+                error = g_own[k, at] * error + (finals[k] - c)
+                base[k, at] = error + c
+            block_e[at] = error
+            return carry
+
+        lax.fori_loop(0, planes, plane, 0)
+
+    @pl.when(s == 0)
+    def _():
+        local_errors(True)
+
+    @pl.when(s == 1)
+    def _():
+        local_errors(False)
+
+    send_all(e_copy)
+    all_p[t] = cum[3, share(t)]
+    all_e[t] = block_e[share(t)]
+
+    def scan(i, state):
+        @pl.when(i != t)
+        def _():
+            remote(
+                cum.at[3, share(i)], all_p.at[i], p_send.at[0], p_recv.at[i], (i, s)
+            ).wait_recv()
+            remote(
+                block_e.at[share(i)], all_e.at[i], e_send.at[0], e_recv.at[i], (i, s)
+            ).wait_recv()
+
+        leave[i] = state
+
+        @pl.when(i != t)
+        def _():
+            x_copy(i, i).start()
+
+        return all_p[i] * state + all_e[i]
+
+    lax.fori_loop(0, n, scan, jnp.zeros((part, lanes), jnp.float32))
+    enter[share(t)] = leave[t]
+
+    def finish(q, carry):
+        @pl.when(q != t)
+        def _():
+            remote(
+                leave.at[q], enter.at[share(q)], x_send.at[q], x_recv.at[q], (q, s)
+            ).wait_recv()
+
+        at = share(q)
+        entering = enter[at]
+        for k in range(4):
+            out_ref[k, at] = base[k, at] + cum[k, at] * entering
+        return carry
+
+    lax.fori_loop(0, n, finish, 0)
+
+    swap_first.wait_send()
+    swap_diff.wait_send()
+    swap_vel.wait_send()
+
+    @pl.when(t < n - 1)
+    def _():
+        to_next.wait_send()
+
+    @pl.when(s == 0)
+    def _():
+        to_upper.wait_send()
+
+    @pl.when((s == 1) & (t == 0))
+    def _():
+        to_lower.wait_send()
+
+    back_first.wait_send()
+    back_second.wait_send()
+
+    def drain(d, carry):
+        peer = lax.rem(t + d, n)
+        p_copy(peer, d).wait_send()
+        e_copy(peer, d).wait_send()
+        x_copy(peer, peer).wait_send()
+        return carry
+
+    lax.fori_loop(1, n, drain, 0)
+
+
+def fused(c_values, initial, diffusivity, velocity, gains):
+    n = lax.axis_size("tm")
+    count, nz, nx, ny = c_values.shape
+    half = nz * nx
+    part = half // n
+    f32 = jnp.float32
+    dma = pltpu.SemaphoreType.DMA
+    field = pltpu.VMEM((2 * half + 2 * nx, ny), f32)
+    block = pltpu.VMEM((half, ny), f32)
+    four = pltpu.VMEM((4, half, ny), f32)
+    shares = pltpu.VMEM((n, part, ny), f32)
+    out = pl.pallas_call(
+        functools.partial(fused_kernel, n, nx, half),
+        out_shape=jax.ShapeDtypeStruct((count, half, ny), f32),
+        in_specs=[pl.BlockSpec(memory_space=pl.ANY)] * 5,
+        out_specs=pl.BlockSpec(memory_space=pltpu.VMEM),
+        scratch_shapes=[
+            four, four,
+            pltpu.VMEM((4, 2 * half, ny), f32),
+            pltpu.VMEM((7, 2 * half, ny), f32),
+            field, field, field,
+            pltpu.VMEM((2, half, ny), f32),
+            four, four, block, shares, shares, shares, block,
+            dma((7,)), dma((3,)), dma((3,)), dma((3,)), dma((2,)), dma((2,)), dma((2,)),
+            dma((n,)), dma((n,)), dma((n,)), dma((n,)), dma((n,)), dma((n,)),
+        ],
+        compiler_params=pltpu.CompilerParams(
+            collective_id=0, has_side_effects=True, vmem_limit_bytes=32 * 1024 * 1024
+        ),
+    )(
+        c_values.reshape(count, half, ny),
+        initial.reshape(half, ny),
+        diffusivity.reshape(half, ny),
+        velocity.reshape(3, half, ny),
+        gains.reshape(count, half, ny),
+    )
+    return out.reshape(c_values.shape)
+
+
+def planned(c_values, initial, diffusivity, velocity, gains):
+    n, slabs = lax.axis_size("tm"), lax.axis_size("slab")
+    count, nz, nx, ny = c_values.shape
+    fits = slabs == 2 and count == 4 and n > 1 and nx % 8 == 0 and ny % 128 == 0
+    if fits and (nz * nx) % (8 * n) == 0:
+        return fused(c_values, initial, diffusivity, velocity, gains)
+    return body(c_values, initial, diffusivity, velocity, gains)
+
+
 def solution(mesh):
     placed = (
         P("tm", "slab", None, None),
@@ -103,5 +493,5 @@
         P("tm", "slab", None, None),
     )
     return jax.shard_map(
-        body, mesh=mesh, in_specs=placed, out_specs=P("tm", "slab", None, None), check_vma=False
-    )
+        planned, mesh=mesh, in_specs=placed, out_specs=P("tm", "slab", None, None), check_vma=False
+    )

time: 210 us -> 30.2 us (0.14)
  the two profiles are of different devices: /device:TPU:24 before, /device:TPU:0 now
where the time goes in v1:
time: 30.2 us; the launch traced here: 29.9 us
  Pallas kernels  24.2 us (80%)
  local copies, waits for them, and re-layouts  5.68 us (19%)
    pallas_call x1, Pallas kernels, fused(): pl.pallas_call(functools.partial(fused_kernel, n, nx, half), out_shape=ja...  24.2 us
    unnamed x11, local copies, waits for them, and re-layouts  5.68 us

profile of v1, /device:TPU:0, one launch (start us, length us, event | category | flops | bytes accessed | tf_op | source)
XLA Modules:
  0.0 29.9 jit_solution(17088938112329997853)
XLA Ops:
  0.0 0.0 copy-start
  0.0 1.0 %copy-done = f32[4,4,64,128]{3,2,1,0:T(8,128)S(1)} copy-done((f32[4,4,64,128]{3,2,1,0:T(8,128)S(1)}, f32[4,4,64,128]{3,2,1,0:T(8,128)}, u32[]{:S(2)}) %copy-start) | copy-done | bytes 524312
  1.0 0.0 copy-start.1
  1.0 1.0 %copy-done.1 = f32[4,4,64,128]{3,2,1,0:T(8,128)S(1)} copy-done((f32[4,4,64,128]{3,2,1,0:T(8,128)S(1)}, f32[4,4,64,128]{3,2,1,0:T(8,128)}, u32[]{:S(2)}) %copy-start.1) | copy-done | bytes 524312
  2.1 0.0 copy-start.2
  2.1 1.0 %copy-done.2 = f32[3,4,64,128]{3,2,1,0:T(8,128)S(1)} copy-done((f32[3,4,64,128]{3,2,1,0:T(8,128)S(1)}, f32[3,4,64,128]{3,2,1,0:T(8,128)}, u32[]{:S(2)}) %copy-start.2) | copy-done | bytes 393240
  3.1 0.0 copy-start.3
  3.1 0.9 %copy-done.3 = f32[4,64,128]{2,1,0:T(8,128)S(1)} copy-done((f32[4,64,128]{2,1,0:T(8,128)S(1)}, f32[4,64,128]{2,1,0:T(8,128)}, u32[]{:S(2)}) %copy-start.3) | copy-done | bytes 131096
  4.0 0.0 copy-start.4
  4.0 0.9 %copy-done.4 = f32[4,64,128]{2,1,0:T(8,128)S(1)} copy-done((f32[4,64,128]{2,1,0:T(8,128)S(1)}, f32[4,64,128]{2,1,0:T(8,128)}, u32[]{:S(2)}) %copy-start.4) | copy-done | bytes 131096
  4.9 24.2 %shard_map.55 = f32[4,256,128]{2,1,0:T(8,128)S(1)} custom-call(f32[4,256,128]{2,1,0:T(8,128)S(1)} %bitcast.7, f32[256,128]{1,0:T(8,128)S(1)} %bitcast.10, f32[256,128]{1,0:T(8,128)S(1)} %bitcast.11, f32[3,256,128]{2,1,0:T(8,128)S(1)} %bitcast.9, f32[4,256,128]{2,1,0:T(8,128)S(1)} %bitcast.8), custom_call_target="tpu_custom_call" | custom-call | tf_op jit(solution)/shard_map/pallas_call | solution.py:450
  29.1 0.8 %copy.7 = f32[4,4,64,128]{3,2,1,0:T(8,128)} copy(f32[4,4,64,128]{3,2,1,0:T(8,128)S(1)} %bitcast.6) | data formatting | bytes 1048576
Async XLA Ops:
  0.0 1.0 %copy-start = (f32[4,4,64,128]{3,2,1,0:T(8,128)S(1)}, f32[4,4,64,128]{3,2,1,0:T(8,128)}, u32[]{:S(2)}) copy-start(f32[4,4,64,128]{3,2,1,0:T(8,128)} %param.5) | copy-start | bytes 1572868
  1.0 1.0 %copy-start.1 = (f32[4,4,64,128]{3,2,1,0:T(8,128)S(1)}, f32[4,4,64,128]{3,2,1,0:T(8,128)}, u32[]{:S(2)}) copy-start(f32[4,4,64,128]{3,2,1,0:T(8,128)} %param.9) | copy-start | bytes 1572868
  2.1 1.0 %copy-start.2 = (f32[3,4,64,128]{3,2,1,0:T(8,128)S(1)}, f32[3,4,64,128]{3,2,1,0:T(8,128)}, u32[]{:S(2)}) copy-start(f32[3,4,64,128]{3,2,1,0:T(8,128)} %param.8) | copy-start | bytes 1179652
  3.1 0.9 %copy-start.3 = (f32[4,64,128]{2,1,0:T(8,128)S(1)}, f32[4,64,128]{2,1,0:T(8,128)}, u32[]{:S(2)}) copy-start(f32[4,64,128]{2,1,0:T(8,128)} %param.6) | copy-start | bytes 393220
  4.0 0.9 %copy-start.4 = (f32[4,64,128]{2,1,0:T(8,128)S(1)}, f32[4,64,128]{2,1,0:T(8,128)}, u32[]{:S(2)}) copy-start(f32[4,64,128]{2,1,0:T(8,128)} %param.7) | copy-start | bytes 393220

commit v2 on v1

--- a/solution.py
+++ b/solution.py
@@ -8,6 +8,7 @@
 from jax.sharding import PartitionSpec as P
 
 STEPS = 8
+GROUP = 4
 MESH = pl.DeviceIdType.MESH
 
 
@@ -103,16 +104,18 @@
     n, nx, half,
     c_hbm, init_hbm, diff_hbm, vel_hbm, gains_hbm, out_ref,
     c_own, g_own, raw, coef, first, second, spare, ends,
-    base, cum, block_e, all_p, all_e, leave, enter,
+    base, cum, block_e, all_p, all_e, leave, enter, below, above,
     local_sem, swap_send, swap_recv, start_send, start_recv, ends_send, ends_recv,
-    p_send, p_recv, e_send, e_recv, x_send, x_recv,
+    p_send, p_recv, e_send, e_recv, x_send, x_recv, up_send, up_recv,
 ):
     t, s = lax.axis_index("tm"), lax.axis_index("slab")
     other = 1 - s
     lanes = c_own.shape[-1]
     planes = half // nx
     whole = 2 * half
-    part = half // n
+    part = half // GROUP
+    member = lax.rem(t, GROUP)
+    leader = t - member
     mine = pl.ds(pl.multiple_of(s * half, half), half)
     theirs = pl.ds(pl.multiple_of(other * half, half), half)
     mine_in = pl.ds(pl.multiple_of(nx + s * half, nx), half)
@@ -123,26 +126,26 @@
     def greet(where):
         pl.semaphore_signal(barrier, inc=1, device_id=where, device_id_type=MESH)
 
-    def hello(d, carry):
-        greet((lax.rem(t + d, n), s))
-        return carry
-
     zero = jnp.zeros((nx, lanes), jnp.float32)
     for field in (first, second, spare):
         field[0:nx] = zero
         field[nx + whole : 2 * nx + whole] = zero
 
     greet((t, other))
+    for d in range(1, GROUP):
+        greet((leader + lax.rem(member + d, GROUP), s))
+
+    @pl.when(t >= GROUP)
+    def _():
+        greet((t - GROUP, s))
 
     @pl.when((s == 0) & (t > 0))
     def _():
-        greet((t - 1, other))
-
-    @pl.when((s == 1) & (t < n - 1))
-    def _():
-        greet((t + 1, other))
-
-    lax.fori_loop(1, n, hello, 0)
+        greet((t - 1, 1))
+
+    @pl.when((s == 0) & (t > 0) & (member == 0))
+    def _():
+        greet((t - 1, 0))
 
     local_diff = pltpu.make_async_copy(diff_hbm, raw.at[0, mine], local_sem.at[0])
     local_vel = pltpu.make_async_copy(vel_hbm, raw.at[1:4, mine], local_sem.at[1])
@@ -166,8 +169,8 @@
     local_g.start()
     local_c.start()
 
-    extra = jnp.where(s == 0, jnp.where(t > 0, 1, 0), jnp.where(t < n - 1, 1, 0))
-    pl.semaphore_wait(barrier, n + extra)
+    later = jnp.where(t < n - GROUP, 1, 0)
+    following = jnp.where((t < n - 1) & ((s == 1) | (member == GROUP - 1)), 1, 0)
 
     def remote(src, dst, send, recv, where):
         return pltpu.make_async_remote_copy(
@@ -189,22 +192,6 @@
     to_lower = remote(
         init_hbm, second.at[mine_in], start_send.at[2], start_recv.at[s], (t, 0)
     )
-
-    @pl.when(t < n - 1)
-    def _():
-        to_next.start()
-
-    swap_diff.start()
-    swap_vel.start()
-    swap_first.start()
-
-    @pl.when(s == 0)
-    def _():
-        to_upper.start()
-
-    @pl.when((s == 1) & (t == 0))
-    def _():
-        to_lower.start()
 
     row = lax.broadcasted_iota(jnp.int32, (nx, lanes), 0)
     lane = lax.broadcasted_iota(jnp.int32, (nx, lanes), 1)
@@ -251,30 +238,50 @@
 
     lax.fori_loop(0, planes, products, 0)
 
+    pl.semaphore_wait(barrier, GROUP + later + following)
+
+    @pl.when(t < n - 1)
+    def _():
+        to_next.start()
+
+    swap_diff.start()
+    swap_vel.start()
+    swap_first.start()
+
+    @pl.when(s == 0)
+    def _():
+        to_upper.start()
+
+    @pl.when((s == 1) & (t == 0))
+    def _():
+        to_lower.start()
+
     def share(q):
         return pl.ds(pl.multiple_of(q * part, part), part)
 
-    def p_copy(peer, index):
+    def p_copy(d):
+        peer = lax.rem(member + d, GROUP)
         return remote(
-            cum.at[3, share(peer)], all_p.at[t], p_send.at[index], p_recv.at[t], (peer, s)
+            cum.at[3, share(peer)], all_p.at[member], p_send.at[d], p_recv.at[member],
+            (leader + peer, s),
         )
 
-    def e_copy(peer, index):
+    def e_copy(d):
+        peer = lax.rem(member + d, GROUP)
         return remote(
-            block_e.at[share(peer)], all_e.at[t], e_send.at[index], e_recv.at[t], (peer, s)
+            block_e.at[share(peer)], all_e.at[member], e_send.at[d], e_recv.at[member],
+            (leader + peer, s),
         )
 
-    def x_copy(peer, index):
+    def x_copy(peer):
         return remote(
-            leave.at[peer], enter.at[share(t)], x_send.at[index], x_recv.at[t], (peer, s)
+            leave.at[peer], enter.at[share(member)], x_send.at[peer], x_recv.at[member],
+            (leader + peer, s),
         )
 
-    def send_all(copy):
-        def one(d, carry):
-            copy(lax.rem(t + d, n), d).start()
-            return carry
-
-        lax.fori_loop(1, n, one, 0)
+    up = remote(above, below, up_send.at[0], up_recv.at[0], (t + GROUP, s))
+    for d in range(1, GROUP):
+        p_copy(d).start()
 
     swap_diff.wait_recv()
     swap_vel.wait_recv()
@@ -304,7 +311,6 @@
 
     local_first.wait()
     swap_first.wait_recv()
-    send_all(p_copy)
     propagated(first)
 
     back_first = remote(
@@ -367,36 +373,58 @@
     def _():
         local_errors(False)
 
-    send_all(e_copy)
-    all_p[t] = cum[3, share(t)]
-    all_e[t] = block_e[share(t)]
-
-    def scan(i, state):
-        @pl.when(i != t)
+    for d in range(1, GROUP):
+        e_copy(d).start()
+    all_p[member] = cum[3, share(member)]
+    all_e[member] = block_e[share(member)]
+    for i in range(GROUP):
+        @pl.when(i != member)
         def _():
             remote(
-                cum.at[3, share(i)], all_p.at[i], p_send.at[0], p_recv.at[i], (i, s)
+                cum.at[3, share(i)], all_p.at[i], p_send.at[0], p_recv.at[i], (leader + i, s)
             ).wait_recv()
             remote(
-                block_e.at[share(i)], all_e.at[i], e_send.at[0], e_recv.at[i], (i, s)
+                block_e.at[share(i)], all_e.at[i], e_send.at[0], e_recv.at[i], (leader + i, s)
             ).wait_recv()
 
-        leave[i] = state
-
-        @pl.when(i != t)
+    total = all_e[0]
+    product = all_p[0]
+    for i in range(1, GROUP):
+        total = all_p[i] * total + all_e[i]
+        product = all_p[i] * product
+
+    @pl.when(t < GROUP)
+    def _():
+        leave[0] = jnp.zeros((part, lanes), jnp.float32)
+
+    @pl.when(t >= GROUP)
+    def _():
+        remote(above, below, up_send.at[0], up_recv.at[0], (leader, other)).wait_recv()
+        leave[0] = below[...]
+
+    above[...] = product * leave[0] + total
+
+    @pl.when(t < n - GROUP)
+    def _():
+        up.start()
+
+    for i in range(GROUP):
+        if i:
+            leave[i] = all_p[i - 1] * leave[i - 1] + all_e[i - 1]
+
+        @pl.when(i != member)
         def _():
-            x_copy(i, i).start()
-
-        return all_p[i] * state + all_e[i]
-
-    lax.fori_loop(0, n, scan, jnp.zeros((part, lanes), jnp.float32))
-    enter[share(t)] = leave[t]
-
-    def finish(q, carry):
-        @pl.when(q != t)
+            x_copy(i).start()
+
+    enter[share(member)] = leave[member]
+
+    def finish(d, carry):
+        q = lax.rem(member + d, GROUP)
+
+        @pl.when(d > 0)
         def _():
             remote(
-                leave.at[q], enter.at[share(q)], x_send.at[q], x_recv.at[q], (q, s)
+                leave.at[q], enter.at[share(q)], x_send.at[q], x_recv.at[q], (leader + q, s)
             ).wait_recv()
 
         at = share(q)
@@ -405,7 +433,7 @@
             out_ref[k, at] = base[k, at] + cum[k, at] * entering
         return carry
 
-    lax.fori_loop(0, n, finish, 0)
+    lax.fori_loop(0, GROUP, finish, 0)
 
     swap_first.wait_send()
     swap_diff.wait_send()
@@ -426,31 +454,32 @@
     back_first.wait_send()
     back_second.wait_send()
 
-    def drain(d, carry):
-        peer = lax.rem(t + d, n)
-        p_copy(peer, d).wait_send()
-        e_copy(peer, d).wait_send()
-        x_copy(peer, peer).wait_send()
-        return carry
-
-    lax.fori_loop(1, n, drain, 0)
+    for d in range(1, GROUP):
+        p_copy(d).wait_send()
+        e_copy(d).wait_send()
+        x_copy(lax.rem(member + d, GROUP)).wait_send()
+
+    @pl.when(t < n - GROUP)
+    def _():
+        up.wait_send()
 
 
 def fused(c_values, initial, diffusivity, velocity, gains):
     n = lax.axis_size("tm")
     count, nz, nx, ny = c_values.shape
     half = nz * nx
-    part = half // n
+    part = half // GROUP
     f32 = jnp.float32
     dma = pltpu.SemaphoreType.DMA
     field = pltpu.VMEM((2 * half + 2 * nx, ny), f32)
     block = pltpu.VMEM((half, ny), f32)
     four = pltpu.VMEM((4, half, ny), f32)
-    shares = pltpu.VMEM((n, part, ny), f32)
+    shares = pltpu.VMEM((GROUP, part, ny), f32)
+    share = pltpu.VMEM((part, ny), f32)
     out = pl.pallas_call(
         functools.partial(fused_kernel, n, nx, half),
         out_shape=jax.ShapeDtypeStruct((count, half, ny), f32),
-        in_specs=[pl.BlockSpec(memory_space=pl.ANY)] * 5,
+        in_specs=[pl.BlockSpec(memory_space=pltpu.HBM)] * 5,
         out_specs=pl.BlockSpec(memory_space=pltpu.VMEM),
         scratch_shapes=[
             four, four,
@@ -458,12 +487,13 @@
             pltpu.VMEM((7, 2 * half, ny), f32),
             field, field, field,
             pltpu.VMEM((2, half, ny), f32),
-            four, four, block, shares, shares, shares, block,
+            four, four, block, shares, shares, shares, block, share, share,
             dma((7,)), dma((3,)), dma((3,)), dma((3,)), dma((2,)), dma((2,)), dma((2,)),
-            dma((n,)), dma((n,)), dma((n,)), dma((n,)), dma((n,)), dma((n,)),
+            dma((GROUP,)), dma((GROUP,)), dma((GROUP,)), dma((GROUP,)), dma((GROUP,)), dma((GROUP,)),
+            dma((1,)), dma((1,)),
         ],
         compiler_params=pltpu.CompilerParams(
-            collective_id=0, has_side_effects=True, vmem_limit_bytes=32 * 1024 * 1024
+            collective_id=0, has_side_effects=True, vmem_limit_bytes=60 * 1024 * 1024
         ),
     )(
         c_values.reshape(count, half, ny),
@@ -478,8 +508,8 @@
 def planned(c_values, initial, diffusivity, velocity, gains):
     n, slabs = lax.axis_size("tm"), lax.axis_size("slab")
     count, nz, nx, ny = c_values.shape
-    fits = slabs == 2 and count == 4 and n > 1 and nx % 8 == 0 and ny % 128 == 0
-    if fits and (nz * nx) % (8 * n) == 0:
+    fits = slabs == 2 and count == 4 and n % GROUP == 0 and nx % 8 == 0 and ny % 128 == 0
+    if fits and (nz * nx) % (8 * GROUP) == 0:
         return fused(c_values, initial, diffusivity, velocity, gains)
     return body(c_values, initial, diffusivity, velocity, gains)
 

time: 30.2 us -> 27.1 us (0.90)
  the two profiles are of different devices: /device:TPU:0 before, /device:TPU:24 now
where the time goes in v2:
time: 27.1 us; the launch traced here: 26.7 us
  Pallas kernels  24.8 us (92%)
  local copies, waits for them, and re-layouts  1.89 us (7%)
    pallas_call x1, Pallas kernels, fused(): pl.pallas_call(functools.partial(fused_kernel, n, nx, half), out_shape=ja...  24.8 us
    unnamed x1, local copies, waits for them, and re-layouts  1.89 us

profile of v2, /device:TPU:24, one launch (start us, length us, event | category | flops | bytes accessed | tf_op | source)
XLA Modules:
  0.0 26.7 jit_solution(5447710197755569576)
XLA Ops:
  0.0 24.8 %shard_map.55 = f32[4,256,128]{2,1,0:T(8,128)} custom-call(f32[4,256,128]{2,1,0:T(8,128)} %bitcast.7, f32[256,128]{1,0:T(8,128)} %bitcast.10, f32[256,128]{1,0:T(8,128)} %bitcast.11, f32[3,256,128]{2,1,0:T(8,128)} %bitcast.9, f32[4,256,128]{2,1,0:T(8,128)} %bitcast.8), custom_call_target="tpu_custom_call" | custom-call | tf_op jit(solution)/shard_map/pallas_call | solution.py:479
  24.8 1.9 %copy.7 = f32[4,4,64,128]{3,2,1,0:T(8,128)} copy(f32[4,4,64,128]{3,2,1,0:T(8,128)} %bitcast.6) | data formatting | bytes 1048576

commit v3 on v2

--- a/solution.py
+++ b/solution.py
@@ -104,9 +104,9 @@
     n, nx, half,
     c_hbm, init_hbm, diff_hbm, vel_hbm, gains_hbm, out_ref,
     c_own, g_own, raw, coef, first, second, spare, ends,
-    base, cum, block_e, all_p, all_e, leave, enter, below, above,
+    base, cum, block_e, all_p, all_e, leave, enter, below_p, below_e, group_p, group_e,
     local_sem, swap_send, swap_recv, start_send, start_recv, ends_send, ends_recv,
-    p_send, p_recv, e_send, e_recv, x_send, x_recv, up_send, up_recv,
+    p_send, p_recv, e_send, e_recv, x_send, x_recv, up_send, up_recv, q_send, q_recv,
 ):
     t, s = lax.axis_index("tm"), lax.axis_index("slab")
     other = 1 - s
@@ -116,6 +116,8 @@
     part = half // GROUP
     member = lax.rem(t, GROUP)
     leader = t - member
+    groups = n // GROUP
+    group = t // GROUP
     mine = pl.ds(pl.multiple_of(s * half, half), half)
     theirs = pl.ds(pl.multiple_of(other * half, half), half)
     mine_in = pl.ds(pl.multiple_of(nx + s * half, nx), half)
@@ -135,9 +137,10 @@
     for d in range(1, GROUP):
         greet((leader + lax.rem(member + d, GROUP), s))
 
-    @pl.when(t >= GROUP)
-    def _():
-        greet((t - GROUP, s))
+    for i in range(groups):
+        @pl.when(i < group)
+        def _():
+            greet((i * GROUP + member, s))
 
     @pl.when((s == 0) & (t > 0))
     def _():
@@ -169,7 +172,7 @@
     local_g.start()
     local_c.start()
 
-    later = jnp.where(t < n - GROUP, 1, 0)
+    later = groups - 1 - group
     following = jnp.where((t < n - 1) & ((s == 1) | (member == GROUP - 1)), 1, 0)
 
     def remote(src, dst, send, recv, where):
@@ -279,9 +282,21 @@
             (leader + peer, s),
         )
 
-    up = remote(above, below, up_send.at[0], up_recv.at[0], (t + GROUP, s))
-    for d in range(1, GROUP):
-        p_copy(d).start()
+    def q_copy(i):
+        return remote(
+            group_p, below_p.at[group], q_send.at[i], q_recv.at[group], (i * GROUP + member, s)
+        )
+
+    def up_copy(i):
+        return remote(
+            group_e, below_e.at[group], up_send.at[i], up_recv.at[group], (i * GROUP + member, s)
+        )
+
+    def to_later(act):
+        for i in range(1, groups):
+            @pl.when(i > group)
+            def _():
+                act(i)
 
     swap_diff.wait_recv()
     swap_vel.wait_recv()
@@ -312,6 +327,8 @@
     local_first.wait()
     swap_first.wait_recv()
     propagated(first)
+    for d in range(1, GROUP):
+        p_copy(d).start()
 
     back_first = remote(
         first.at[theirs_in], ends.at[1], ends_send.at[0], ends_recv.at[0], (t, other)
@@ -345,6 +362,19 @@
     )
     back_second.start()
     local_c.wait()
+    all_p[member] = cum[3, share(member)]
+    for i in range(GROUP):
+        @pl.when(i != member)
+        def _():
+            remote(
+                cum.at[3, share(i)], all_p.at[i], p_send.at[0], p_recv.at[i], (leader + i, s)
+            ).wait_recv()
+
+    product = all_p[0]
+    for i in range(1, GROUP):
+        product = all_p[i] * product
+    group_p[...] = product
+    to_later(lambda i: q_copy(i).start())
     back_first.wait_recv()
     back_second.wait_recv()
 
@@ -359,7 +389,7 @@
             for k in range(4):
                 c = c_own[k, at]
                 error = g_own[k, at] * error + (finals[k] - c)
-                base[k, at] = error + c
+                base[k, at] = error
             block_e[at] = error
             return carry
 
@@ -375,38 +405,30 @@
 
     for d in range(1, GROUP):
         e_copy(d).start()
-    all_p[member] = cum[3, share(member)]
     all_e[member] = block_e[share(member)]
     for i in range(GROUP):
         @pl.when(i != member)
         def _():
             remote(
-                cum.at[3, share(i)], all_p.at[i], p_send.at[0], p_recv.at[i], (leader + i, s)
+                block_e.at[share(i)], all_e.at[i], e_send.at[0], e_recv.at[i], (leader + i, s)
+            ).wait_recv()
+
+    total = all_e[0]
+    for i in range(1, GROUP):
+        total = all_p[i] * total + all_e[i]
+    group_e[...] = total
+    to_later(lambda i: up_copy(i).start())
+    leave[0] = jnp.zeros((part, lanes), jnp.float32)
+    for i in range(groups - 1):
+        @pl.when(i < group)
+        def _():
+            remote(
+                group_p, below_p.at[i], q_send.at[0], q_recv.at[i], (i * GROUP + member, s)
             ).wait_recv()
             remote(
-                block_e.at[share(i)], all_e.at[i], e_send.at[0], e_recv.at[i], (leader + i, s)
+                group_e, below_e.at[i], up_send.at[0], up_recv.at[i], (i * GROUP + member, s)
             ).wait_recv()
-
-    total = all_e[0]
-    product = all_p[0]
-    for i in range(1, GROUP):
-        total = all_p[i] * total + all_e[i]
-        product = all_p[i] * product
-
-    @pl.when(t < GROUP)
-    def _():
-        leave[0] = jnp.zeros((part, lanes), jnp.float32)
-
-    @pl.when(t >= GROUP)
-    def _():
-        remote(above, below, up_send.at[0], up_recv.at[0], (leader, other)).wait_recv()
-        leave[0] = below[...]
-
-    above[...] = product * leave[0] + total
-
-    @pl.when(t < n - GROUP)
-    def _():
-        up.start()
+            leave[0] = below_p[i] * leave[0] + below_e[i]
 
     for i in range(GROUP):
         if i:
@@ -459,9 +481,8 @@
         e_copy(d).wait_send()
         x_copy(lax.rem(member + d, GROUP)).wait_send()
 
-    @pl.when(t < n - GROUP)
-    def _():
-        up.wait_send()
+    to_later(lambda i: q_copy(i).wait_send())
+    to_later(lambda i: up_copy(i).wait_send())
 
 
 def fused(c_values, initial, diffusivity, velocity, gains):
@@ -476,7 +497,9 @@
     four = pltpu.VMEM((4, half, ny), f32)
     shares = pltpu.VMEM((GROUP, part, ny), f32)
     share = pltpu.VMEM((part, ny), f32)
-    out = pl.pallas_call(
+    groups = n // GROUP
+    belows = pltpu.VMEM((groups, part, ny), f32)
+    error = pl.pallas_call(
         functools.partial(fused_kernel, n, nx, half),
         out_shape=jax.ShapeDtypeStruct((count, half, ny), f32),
         in_specs=[pl.BlockSpec(memory_space=pltpu.HBM)] * 5,
@@ -487,10 +510,10 @@
             pltpu.VMEM((7, 2 * half, ny), f32),
             field, field, field,
             pltpu.VMEM((2, half, ny), f32),
-            four, four, block, shares, shares, shares, block, share, share,
+            four, four, block, shares, shares, shares, block, belows, belows, share, share,
             dma((7,)), dma((3,)), dma((3,)), dma((3,)), dma((2,)), dma((2,)), dma((2,)),
             dma((GROUP,)), dma((GROUP,)), dma((GROUP,)), dma((GROUP,)), dma((GROUP,)), dma((GROUP,)),
-            dma((1,)), dma((1,)),
+            dma((groups,)), dma((groups,)), dma((groups,)), dma((groups,)),
         ],
         compiler_params=pltpu.CompilerParams(
             collective_id=0, has_side_effects=True, vmem_limit_bytes=60 * 1024 * 1024
@@ -502,7 +525,7 @@
         velocity.reshape(3, half, ny),
         gains.reshape(count, half, ny),
     )
-    return out.reshape(c_values.shape)
+    return c_values + error.reshape(c_values.shape)
 
 
 def planned(c_values, initial, diffusivity, velocity, gains):

time: 27.1 us -> 26 us (0.959)
  other arithmetic: 0 us -> 1.9 us
  local copies, waits for them, and re-layouts: 1.89 us -> 0.01 us
  Pallas kernels: 24.8 us -> 23.9 us
    add x0 -> x1, other arithmetic: none -> 1.9 us  [fused(): return c_values + error.reshape(c_values.shape)]
    unnamed x1 -> x2, local copies, waits for them, and re-layouts: 1.89 us -> 0.01 us
    pallas_call x1, Pallas kernels: 24.8 us -> 23.9 us  [fused(): pl.pallas_call(functools.partial(fused_kernel, n, nx, half), out_shape=ja...]
where the time goes in v3:
time: 26 us; the launch traced here: 25.8 us
  Pallas kernels  23.9 us (92%)
  other arithmetic  1.9 us (7%)
    pallas_call x1, Pallas kernels, fused(): pl.pallas_call(functools.partial(fused_kernel, n, nx, half), out_shape=ja...  23.9 us
    add x1, other arithmetic, fused(): return c_values + error.reshape(c_values.shape)  1.9 us

profile of v3, /device:TPU:24, one launch (start us, length us, event | category | flops | bytes accessed | tf_op | source)
XLA Modules:
  0.0 25.8 jit_solution(2758284314148801529)
XLA Ops:
  0.0 0.0 copy-start
  0.0 23.9 %shard_map.55 = f32[4,256,128]{2,1,0:T(8,128)} custom-call(f32[4,256,128]{2,1,0:T(8,128)} %bitcast.6, f32[256,128]{1,0:T(8,128)} %bitcast.10, f32[256,128]{1,0:T(8,128)} %bitcast.11, f32[3,256,128]{2,1,0:T(8,128)} %bitcast.9, f32[4,256,128]{2,1,0:T(8,128)} %bitcast.8), custom_call_target="tpu_custom_call" | custom-call | tf_op jit(solution)/shard_map/pallas_call | solution.py:502
  23.9 0.0 copy-done
  23.9 1.9 %add.3 = f32[4,4,64,128]{3,2,1,0:T(8,128)} add(f32[4,4,64,128]{3,2,1,0:T(8,128)S(1)} %copy-done, f32[4,4,64,128]{3,2,1,0:T(8,128)} %bitcast.7) | non-fusion elementwise | flops 131072 | bytes 1572864 | tf_op jit(solution)/shard_map/add | solution.py:528
Async XLA Ops:
  0.0 23.9 %copy-start = (f32[4,4,64,128]{3,2,1,0:T(8,128)S(1)}, f32[4,4,64,128]{3,2,1,0:T(8,128)}, u32[]{:S(2)}) copy-start(f32[4,4,64,128]{3,2,1,0:T(8,128)} %param.5) | copy-start | bytes 1572868

commit v4 on v3

--- a/solution.py
+++ b/solution.py
@@ -516,14 +516,14 @@
             dma((groups,)), dma((groups,)), dma((groups,)), dma((groups,)),
         ],
         compiler_params=pltpu.CompilerParams(
-            collective_id=0, has_side_effects=True, vmem_limit_bytes=60 * 1024 * 1024
+            collective_id=0, has_side_effects=True, vmem_limit_bytes=32 * 1024 * 1024
         ),
     )(
-        c_values.reshape(count, half, ny),
-        initial.reshape(half, ny),
-        diffusivity.reshape(half, ny),
-        velocity.reshape(3, half, ny),
-        gains.reshape(count, half, ny),
+        pltpu.with_memory_space_constraint(c_values.reshape(count, half, ny), pltpu.HBM),
+        pltpu.with_memory_space_constraint(initial.reshape(half, ny), pltpu.HBM),
+        pltpu.with_memory_space_constraint(diffusivity.reshape(half, ny), pltpu.HBM),
+        pltpu.with_memory_space_constraint(velocity.reshape(3, half, ny), pltpu.HBM),
+        pltpu.with_memory_space_constraint(gains.reshape(count, half, ny), pltpu.HBM),
     )
     return c_values + error.reshape(c_values.shape)
 

time: 26 us -> 24.1 us (0.927)
  other arithmetic: 1.9 us -> 0.86 us
  Pallas kernels: 23.9 us -> 23.1 us
    add x1, other arithmetic: 1.9 us -> 0.86 us  [fused(): return c_values + error.reshape(c_values.shape)]
    pallas_call x1, Pallas kernels: 23.9 us -> 23.1 us  [fused(): pl.pallas_call(functools.partial(fused_kernel, n, nx, half), out_shape=ja...]
where the time goes in v4:
time: 24.1 us; the launch traced here: 24 us
  Pallas kernels  23.1 us (96%)
  other arithmetic  0.86 us (4%)
    pallas_call x1, Pallas kernels, fused(): pl.pallas_call(functools.partial(fused_kernel, n, nx, half), out_shape=ja...  23.1 us
    add x1, other arithmetic, fused(): return c_values + error.reshape(c_values.shape)  0.86 us

profile of v4, /device:TPU:24, one launch (start us, length us, event | category | flops | bytes accessed | tf_op | source)
XLA Modules:
  0.0 24.0 jit_solution(9786371679751993689)
XLA Ops:
  0.0 0.0 copy-start
  0.0 23.1 %shard_map.55 = f32[4,256,128]{2,1,0:T(8,128)S(1)} custom-call(f32[4,256,128]{2,1,0:T(8,128)} %bitcast.7, f32[256,128]{1,0:T(8,128)} %bitcast.10, f32[256,128]{1,0:T(8,128)} %bitcast.11, f32[3,256,128]{2,1,0:T(8,128)} %bitcast.9, f32[4,256,128]{2,1,0:T(8,128)} %bitcast.8), custom_call_target="tpu_custom_call" | custom-call | tf_op jit(solution)/shard_map/pallas_call | solution.py:502
  23.1 0.0 copy-done
  23.1 0.9 %add.3 = f32[4,4,64,128]{3,2,1,0:T(8,128)} add(f32[4,4,64,128]{3,2,1,0:T(8,128)S(1)} %copy-done, f32[4,4,64,128]{3,2,1,0:T(8,128)S(1)} %bitcast.6) | non-fusion elementwise | flops 131072 | bytes 1572864 | tf_op jit(solution)/shard_map/add | solution.py:528
Async XLA Ops:
  0.0 23.1 %copy-start = (f32[4,4,64,128]{3,2,1,0:T(8,128)S(1)}, f32[4,4,64,128]{3,2,1,0:T(8,128)}, u32[]{:S(2)}) copy-start(f32[4,4,64,128]{3,2,1,0:T(8,128)} %param.5) | copy-start | bytes 1572868
